TPU v7x, 32 devices: a whole 2x2x4 slice. The times are simulated.
32 devices in a mesh: chan: 16 (over z, x, core), win: 2 (over y).
Axes of the slice: x: 2, y: 2, z: 4, core: 2. Of those that a mesh axis runs over, the one named last changes fastest.
Arguments:
- spectra: bfloat16 [2, 4, 2048, 4096], P(None, 'win', 'chan'), may hold values from -6 to 6
- exponents: int32 [4, 2048, 32], P('win', 'chan'), may hold values from -1 to 1
- source_channels: int32 [1], replicated, may hold values from 0 to 2047
Outputs:
- correlations: float32 [1, 2048, 2048], P(None, 'chan', 'win')
All inputs are finite; a program needn't handle non-finite values.
Results may differ from a plain program's by a relative error of at most 0.0003.
Values sent between devices are 32-bit elements; how exact they have to be, the bound alone decides.
A program may use at most 64 MiB of HBM per device.

v0:
```python
import functools
import math

import jax
import jax.numpy as jnp
import ml_dtypes
import numpy as np
from jax import lax
from jax.experimental import pallas as pl
from jax.experimental.pallas import tpu as pltpu
from jax.sharding import PartitionSpec as P

L = 2048
FOLD = 8
CLASSES = 2 * FOLD
LANES = 128
PACK = 16
MESH = pl.DeviceIdType.MESH


def lag_tables(nbin, norm):
    width = nbin // FOLD
    steps = L // CLASSES
    tau = np.arange(CLASSES)[:, None] + CLASSES * (np.arange(steps) - steps // 2)[None, :]
    phase = (tau[:, :, None] * np.arange(width)[None, None, :]) % (2 * nbin)
    angle = phase * (2.0 * math.pi / (2 * nbin))
    full = np.concatenate([np.cos(angle), -np.sin(angle)], axis=2) * norm
    high = full.astype(np.float32).astype(ml_dtypes.bfloat16)
    low = (full - high.astype(np.float64)).astype(np.float32).astype(ml_dtypes.bfloat16)
    return np.concatenate([high, low], axis=1)


def turn(value, eighths):
    re, im = value
    k = eighths % 16
    if k == 0:
        return re, im
    if k == 4:
        return -im, re
    if k == 8:
        return -re, -im
    if k == 12:
        return im, -re
    if k == 2:
        c = math.sqrt(0.5)
        return (re - im) * c, (re + im) * c
    if k == 6:
        c = math.sqrt(0.5)
        return (re + im) * -c, (re - im) * c
    c, s = math.cos(math.pi * k / 8), math.sin(math.pi * k / 8)
    return re * c - im * s, re * s + im * c


def dft(values):
    n = len(values)
    if n == 1:
        return values
    even, odd = dft(values[0::2]), dft(values[1::2])
    odd = [turn(v, 16 // n * k) for k, v in enumerate(odd)]
    low = [(a[0] + b[0], a[1] + b[1]) for a, b in zip(even, odd)]
    high = [(a[0] - b[0], a[1] - b[1]) for a, b in zip(even, odd)]
    return low + high


def kernel(nch, nwin, src_ref, exp_ref, spec_hbm, tab_hbm, out_ref,
           spec, tab, pick, got, mine, slab, folded, part, come, acc,
           spec_sem, tab_sem, s1, r1, s2, r2, s3, r3):
    chan, win = lax.axis_index("chan"), lax.axis_index("win")
    segs, rows, nbin = spec.shape[1], spec.shape[2], spec.shape[3]
    blocks = nbin // LANES
    per = slab.shape[1]
    width = nbin // FOLD
    jblocks = width // LANES
    steps = L // CLASSES
    mine_steps = steps // nwin

    load = pltpu.make_async_copy(spec_hbm, spec, spec_sem)
    load.start()
    load_tab = pltpu.make_async_copy(tab_hbm, tab, tab_sem)
    load_tab.start()

    barrier = pltpu.get_barrier_semaphore()

    @pl.loop(1, nch)
    def _(d):
        pl.semaphore_signal(barrier, inc=1, device_id=(lax.rem(chan + d, nch), win), device_id_type=MESH)

    @pl.loop(1, nwin)
    def _(d):
        pl.semaphore_signal(barrier, inc=1, device_id=(chan, lax.rem(win + d, nwin)), device_id_type=MESH)

    load.wait()
    local = src_ref[0] - chan * rows
    line = lax.broadcasted_iota(jnp.int32, (rows, LANES), 0)
    hits = (line == local).astype(jnp.float32)
    groups = rows // PACK
    marks = [hits[i * PACK : (i + 1) * PACK].astype(jnp.bfloat16) for i in range(groups)]
    for g in range(segs):
        scale = jnp.sum(jnp.exp2(exp_ref[g].astype(jnp.float32)) * hits[:, :blocks], axis=0, keepdims=True)
        for b in range(blocks):
            wide = jnp.broadcast_to(scale[:, b : b + 1], (1, LANES))
            for plane in range(2):
                x = None
                for i in range(groups):
                    y = spec[plane, g, i * PACK : (i + 1) * PACK, b * LANES : (b + 1) * LANES] * marks[i]
                    x = y if x is None else x + y
                row = (plane * segs + g) * blocks + b
                one = jnp.sum(x.astype(jnp.float32), axis=0, keepdims=True)
                pick[row // per, row % per : row % per + 1, :] = one * wide

    pl.semaphore_wait(barrier, nch + nwin - 2)

    def scatter(d):
        to = lax.rem(chan + d, nch)
        return pltpu.make_async_remote_copy(
            src_ref=pick.at[to], dst_ref=got.at[d], send_sem=s1.at[d], recv_sem=r1.at[d],
            device_id=(to, win), device_id_type=MESH)

    def gather(d):
        to = lax.rem(chan + d, nch)
        return pltpu.make_async_remote_copy(
            src_ref=mine, dst_ref=slab.at[chan], send_sem=s2.at[d], recv_sem=r2.at[d],
            device_id=(to, win), device_id_type=MESH)

    @pl.loop(1, nch)
    def _(d):
        scatter(d).start()

    total = pick[chan]
    for d in range(1, nch):
        scatter(d).wait_recv()
        total = total + got[d]
    mine[...] = total
    slab[chan] = total

    @pl.loop(1, nch)
    def _(d):
        gather(d).start()

    @pl.loop(0, rows // PACK)
    def _(i):
        here = pl.ds(pl.multiple_of(i * PACK, PACK), PACK)
        for g in range(segs):
            scale = jnp.exp2(exp_ref[g, here, :].astype(jnp.float32))
            for b in range(blocks):
                wide = jnp.broadcast_to(scale[:, b : b + 1], (PACK, LANES))
                cut = slice(b * LANES, (b + 1) * LANES)
                for plane in range(2):
                    x = spec[plane, g, here, cut].astype(jnp.float32)
                    spec[plane, g, here, cut] = (x * wide).astype(jnp.bfloat16)

    @pl.loop(1, nch)
    def _(d):
        gather(d).wait_recv()

    @pl.loop(0, rows // PACK)
    def _(i):
        start = pl.multiple_of(i * PACK, PACK)
        here = pl.ds(start, PACK)
        below = pl.ds(pl.multiple_of(rows + start, PACK), PACK)
        for j in range(jblocks):
            cross = []
            for h in range(FOLD):
                b = h * jblocks + j
                cut = slice(b * LANES, (b + 1) * LANES)
                re = im = None
                for g in range(segs):
                    ra, rb = g * blocks + b, (segs + g) * blocks + b
                    sr = slab[ra // per, ra % per : ra % per + 1, :]
                    si = slab[rb // per, rb % per : rb % per + 1, :]
                    xr = spec[0, g, here, cut].astype(jnp.float32)
                    xi = spec[1, g, here, cut].astype(jnp.float32)
                    tr, ti = sr * xr + si * xi, sr * xi - si * xr
                    re, im = (tr, ti) if re is None else (re + tr, im + ti)
                cross.append((re, im))
            for odd in range(2):
                if odd:
                    cross = [turn(v, h) for h, v in enumerate(cross)]
                for m, pair in enumerate(dft(cross)):
                    for plane in range(2):
                        cut = slice(plane * width + j * LANES, plane * width + (j + 1) * LANES)
                        high = pair[plane].astype(jnp.bfloat16)
                        low = (pair[plane] - high.astype(jnp.float32)).astype(jnp.bfloat16)
                        folded[2 * m + odd, here, cut] = high
                        folded[2 * m + odd, below, cut] = low

    load_tab.wait()

    def give(k, d):
        to = lax.rem(win + d, nwin)
        return pltpu.make_async_remote_copy(
            src_ref=part.at[k, to], dst_ref=come.at[d - 1, k], send_sem=s3.at[k, d - 1],
            recv_sem=r3.at[k, d - 1], device_id=(chan, to), device_id_type=MESH)

    @pl.loop(0, CLASSES)
    def _(k):
        r = lax.dot_general(tab[k], folded[k], (((1,), (1,)), ((), ())),
                            preferred_element_type=jnp.float32)
        low = r[:steps, rows:] + r[steps:, :rows] + r[steps:, rows:]
        part[k] = (r[:steps, :rows] + low).reshape(nwin, mine_steps, rows)
        for d in range(1, nwin):
            give(k, d).start()

    @pl.loop(1, nch)
    def _(d):
        scatter(d).wait_send()
        gather(d).wait_send()

    for k in range(CLASSES):
        value = part[k, win]
        for d in range(1, nwin):
            give(k, d).wait_recv()
            value = value + come[d - 1, k]
        acc[pl.ds(k, mine_steps, stride=CLASSES), :] = value

    for t in range(L // nwin // LANES):
        cut = slice(t * LANES, (t + 1) * LANES)
        out_ref[:, cut] = acc[cut, :].T

    @pl.loop(0, CLASSES)
    def _(k):
        for d in range(1, nwin):
            give(k, d).wait_send()


def body(spectra, exponents, source_channels):
    nch, nwin = lax.axis_size("chan"), lax.axis_size("win")
    _, segs, rows, nbin = spectra.shape
    per = 2 * segs * nbin // LANES // nch
    steps = L // CLASSES
    width = nbin // FOLD
    tables = jnp.asarray(lag_tables(nbin, 1.0 / math.sqrt(4.0 * nbin * segs * nwin)))
    f32, bf16, dma = jnp.float32, jnp.bfloat16, pltpu.SemaphoreType.DMA
    call = pl.pallas_call(
        functools.partial(kernel, nch, nwin),
        out_shape=jax.ShapeDtypeStruct((rows, L // nwin), f32),
        in_specs=[
            pl.BlockSpec(memory_space=pltpu.SMEM),
            pl.BlockSpec(memory_space=pltpu.VMEM),
            pl.BlockSpec(memory_space=pl.ANY),
            pl.BlockSpec(memory_space=pl.ANY),
        ],
        out_specs=pl.BlockSpec(memory_space=pltpu.VMEM),
        scratch_shapes=[
            pltpu.VMEM(spectra.shape, bf16),
            pltpu.VMEM((CLASSES, 2 * steps, 2 * width), bf16),
            pltpu.VMEM((nch, per, LANES), f32),
            pltpu.VMEM((nch, per, LANES), f32),
            pltpu.VMEM((per, LANES), f32),
            pltpu.VMEM((nch, per, LANES), f32),
            pltpu.VMEM((CLASSES, 2 * rows, 2 * width), bf16),
            pltpu.VMEM((CLASSES, nwin, steps // nwin, rows), f32),
            pltpu.VMEM((nwin - 1, CLASSES, steps // nwin, rows), f32),
            pltpu.VMEM((L // nwin, rows), f32),
            dma, dma,
            dma((nch,)), dma((nch,)), dma((nch,)), dma((nch,)),
            dma((CLASSES, nwin - 1)), dma((CLASSES, nwin - 1)),
        ],
        compiler_params=pltpu.CompilerParams(
            collective_id=0, has_side_effects=True, vmem_limit_bytes=48 * 2**20),
    )
    out = [call(source_channels[s : s + 1], exponents, spectra, tables)
           for s in range(source_channels.shape[0])]
    return jnp.stack(out)


def solution(mesh):
    return jax.shard_map(
        body,
        mesh=mesh,
        in_specs=(P(None, "win", "chan", None), P("win", "chan", None), P()),
        out_specs=P(None, "chan", "win"),
        check_vma=False,
    )
```

profile of v0, /device:TPU:0, one launch (start us, length us, event | category | flops | bytes accessed | tf_op | source)
XLA Modules:
  0.0 38.4 jit_solution(15990542253672787962)
XLA Ops:
  0.7 0.9 %copy.5.exp_ref = s32[2,128,32]{2,1,0:T(8,128)S(1)} copy(s32[2,128,32]{1,2,0:T(8,128)} %param.5) | data formatting | bytes 65536 | tf_op args[1]
  1.5 0.0 copy-start
  1.5 2.2 %copy-done = bf16[2,2,128,4096]{3,2,1,0:T(8,128)(2,1)S(1)} copy-done((bf16[2,2,128,4096]{3,2,1,0:T(8,128)(2,1)S(1)}, bf16[2,2,128,4096]{3,2,1,0:T(8,128)(2,1)}, u32[]{:S(2)}) %copy-start) | copy-done | bytes 4194328
  3.7 33.9 %shard_map.46 = f32[128,1024]{1,0:T(8,128)S(1)} custom-call(s32[1]{0:T(128)S(6)} %copy.7.src_ref, s32[2,128,32]{2,1,0:T(8,128)S(1)} %copy.5.exp_ref, bf16[2,2,128,4096]{3,2,1,0:T(8,128)(2,1)S(1)} %copy-done, bf16[16,256,1024]{2,1,0:T(8,128)(2,1)} %constant.2.clone.tab_hbm), custom_call_target="tpu_custom_call" | custom-call | tf_op jit(solution)/shard_map/pallas_call | solution.py:262
  37.6 0.8 %copy.8 = f32[1,128,1024]{2,1,0:T(8,128)} copy(f32[1,128,1024]{2,1,0:T(8,128)S(1)} %bitcast.1) | data formatting | bytes 1048576
Async XLA Ops:
  1.5 2.2 %copy-start = (bf16[2,2,128,4096]{3,2,1,0:T(8,128)(2,1)S(1)}, bf16[2,2,128,4096]{3,2,1,0:T(8,128)(2,1)}, u32[]{:S(2)}) copy-start(bf16[2,2,128,4096]{3,2,1,0:T(8,128)(2,1)} %spec_hbm.1) | copy-start | bytes 12582916
where the time goes:
time: 38.7 us; the launch traced here: 38.4 us
  Pallas kernels  33.9 us (88%)
  local copies, waits for them, and re-layouts  3.84 us (10%)
  between operations  0.67 us (2%)
    pallas_call x1, Pallas kernels, body(): call(source_channels[s:s + 1], exponents, spectra, tables)  33.9 us
    unnamed x4, local copies, waits for them, and re-layouts  3.84 us

commit v1 on v0

v1 whole, which is shorter than its diff:
```python
import functools
import math

import jax
import jax.numpy as jnp
import ml_dtypes
import numpy as np
from jax import lax
from jax.experimental import pallas as pl
from jax.experimental.pallas import tpu as pltpu
from jax.sharding import PartitionSpec as P

L = 2048
FOLD = 8
CLASSES = 2 * FOLD
LANES = 128
PACK = 16
NEAR = 4
MESH = pl.DeviceIdType.MESH


def lag_tables(nbin, norm):
    width = nbin // FOLD
    steps = L // CLASSES
    tau = np.arange(CLASSES)[:, None] + CLASSES * (np.arange(steps) - steps // 2)[None, :]
    phase = (tau[:, :, None] * np.arange(width)[None, None, :]) % (2 * nbin)
    angle = phase * (2.0 * math.pi / (2 * nbin))
    full = np.concatenate([np.cos(angle), -np.sin(angle)], axis=2) * norm
    high = full.astype(np.float32).astype(ml_dtypes.bfloat16)
    low = (full - high.astype(np.float64)).astype(np.float32).astype(ml_dtypes.bfloat16)
    return np.concatenate([high, low], axis=1)


def turn(value, eighths):
    re, im = value
    k = eighths % 16
    if k == 0:
        return re, im
    if k == 4:
        return -im, re
    if k == 8:
        return -re, -im
    if k == 12:
        return im, -re
    if k == 2:
        c = math.sqrt(0.5)
        return (re - im) * c, (re + im) * c
    if k == 6:
        c = math.sqrt(0.5)
        return (re + im) * -c, (re - im) * c
    c, s = math.cos(math.pi * k / 8), math.sin(math.pi * k / 8)
    return re * c - im * s, re * s + im * c


def dft(values):
    n = len(values)
    if n == 1:
        return values
    even, odd = dft(values[0::2]), dft(values[1::2])
    odd = [turn(v, 16 // n * k) for k, v in enumerate(odd)]
    low = [(a[0] + b[0], a[1] + b[1]) for a, b in zip(even, odd)]
    high = [(a[0] - b[0], a[1] - b[1]) for a, b in zip(even, odd)]
    return low + high


def kernel(nch, nwin, src_ref, exp_hbm, spec_hbm, tab_hbm, out_ref,
           spec, tab, vals, raw, scales, pick, got, mine, got2, total, slab, even, odd,
           part, come, acc,
           spec_sem, tab_sem, exp_sem, s1, r1, s2, r2, s4, r4, s3, r3):
    chan, win = lax.axis_index("chan"), lax.axis_index("win")
    segs, rows, nbin = spec.shape[1], spec.shape[2], spec.shape[3]
    blocks = nbin // LANES
    per = slab.shape[1]
    width = nbin // FOLD
    jblocks = width // LANES
    steps = L // CLASSES
    mine_steps = steps // nwin

    load_exp = pltpu.make_async_copy(exp_hbm, raw, exp_sem)
    load_exp.start()
    load = pltpu.make_async_copy(spec_hbm, spec, spec_sem)
    load.start()
    load_tab = pltpu.make_async_copy(tab_hbm, tab, tab_sem)

    near, far = lax.rem(chan, NEAR), lax.div(chan, NEAR)
    nfar = nch // NEAR

    def beside(d):
        return lax.rem(near + d, NEAR)

    def ahead(d):
        return lax.rem(far + d, nfar) * NEAR + near

    barrier = pltpu.get_barrier_semaphore()
    for d in range(1, NEAR):
        pl.semaphore_signal(barrier, inc=1, device_id=(far * NEAR + beside(d), win), device_id_type=MESH)

    @pl.loop(1, nfar)
    def _(d):
        pl.semaphore_signal(barrier, inc=1, device_id=(ahead(d), win), device_id_type=MESH)

    @pl.loop(1, nwin)
    def _(d):
        pl.semaphore_signal(barrier, inc=1, device_id=(chan, lax.rem(win + d, nwin)), device_id_type=MESH)

    load_exp.wait()
    flat = jnp.exp2(raw[...].astype(jnp.float32)).reshape(segs * blocks, rows)
    square = jnp.concatenate([flat, jnp.ones((LANES - segs * blocks, rows), jnp.float32)], axis=0)
    scales[...] = square.T
    load.wait()
    load_tab.start()
    local = src_ref[0] - chan * rows
    line = lax.broadcasted_iota(jnp.int32, (rows, LANES), 0)
    hits = (line == local).astype(jnp.float32)
    groups = rows // PACK
    marks = [hits[i * PACK : (i + 1) * PACK].astype(jnp.bfloat16) for i in range(groups)]
    scale = jnp.sum(scales[...] * hits, axis=0, keepdims=True)
    for g in range(segs):
        for b in range(blocks):
            wide = jnp.broadcast_to(scale[:, g * blocks + b : g * blocks + b + 1], (1, LANES))
            for plane in range(2):
                x = None
                for i in range(groups):
                    y = spec[plane, g, i * PACK : (i + 1) * PACK, b * LANES : (b + 1) * LANES] * marks[i]
                    x = y if x is None else x + y
                row = (plane * segs + g) * blocks + b
                one = jnp.sum(x.astype(jnp.float32), axis=0, keepdims=True)
                pick[row // per, row % per : row % per + 1, :] = one * wide

    pl.semaphore_wait(barrier, NEAR + nfar + nwin - 3)

    def scatter(d):
        to = beside(d)
        return pltpu.make_async_remote_copy(
            src_ref=pick.at[to], dst_ref=got.at[d], send_sem=s1.at[d], recv_sem=r1.at[d],
            device_id=(far * NEAR + to, win), device_id_type=MESH)

    def across(d):
        return pltpu.make_async_remote_copy(
            src_ref=mine, dst_ref=got2.at[d], send_sem=s2.at[d], recv_sem=r2.at[d],
            device_id=(ahead(d), win), device_id_type=MESH)

    def gather(d):
        return pltpu.make_async_remote_copy(
            src_ref=total, dst_ref=slab.at[near], send_sem=s4.at[d], recv_sem=r4.at[d],
            device_id=(far * NEAR + beside(d), win), device_id_type=MESH)

    for d in range(1, NEAR):
        scatter(d).start()
    added = pick[near]
    for d in range(1, NEAR):
        scatter(d).wait_recv()
        added = added + got[d]
    mine[...] = added
    for d in range(1, nfar):
        across(d).start()

    @pl.loop(0, rows // PACK)
    def _(i):
        here = pl.ds(pl.multiple_of(i * PACK, PACK), PACK)
        scale = scales[here, :]
        for g in range(segs):
            for b in range(blocks):
                wide = jnp.broadcast_to(scale[:, g * blocks + b : g * blocks + b + 1], (PACK, LANES))
                cut = slice(b * LANES, (b + 1) * LANES)
                for plane in range(2):
                    x = spec[plane, g, here, cut].astype(jnp.float32)
                    vals[plane, g, here, cut] = x * wide

    for d in range(1, nfar):
        across(d).wait_recv()
        added = added + got2[d]
    total[...] = added
    slab[near] = added
    for d in range(1, NEAR):
        gather(d).start()
    for d in range(1, NEAR):
        gather(d).wait_recv()

    def split(folded, pairs, j, here, below):
        for m, pair in enumerate(dft(pairs)):
            for plane in range(2):
                cut = slice(plane * width + j * LANES, plane * width + (j + 1) * LANES)
                high = pair[plane].astype(jnp.bfloat16)
                low = (pair[plane] - high.astype(jnp.float32)).astype(jnp.bfloat16)
                folded[m, here, cut] = high
                folded[m, below, cut] = low

    def spots(i):
        start = pl.multiple_of(i * PACK, PACK)
        return pl.ds(start, PACK), pl.ds(pl.multiple_of(rows + start, PACK), PACK)

    @pl.loop(0, rows // PACK)
    def _(i):
        here, below = spots(i)
        for j in range(jblocks):
            cross = []
            for h in range(FOLD):
                b = h * jblocks + j
                cut = slice(b * LANES, (b + 1) * LANES)
                re = im = None
                for g in range(segs):
                    ra, rb = g * blocks + b, (segs + g) * blocks + b
                    sr = slab[ra // per, ra % per : ra % per + 1, :]
                    si = slab[rb // per, rb % per : rb % per + 1, :]
                    xr, xi = vals[0, g, here, cut], vals[1, g, here, cut]
                    tr, ti = sr * xr + si * xi, sr * xi - si * xr
                    re, im = (tr, ti) if re is None else (re + tr, im + ti)
                vals[0, 0, here, cut] = re
                vals[1, 0, here, cut] = im
                cross.append((re, im))
            split(even, cross, j, here, below)

    def fold_odd(i):
        here, below = spots(i)
        for j in range(jblocks):
            turned = []
            for h in range(FOLD):
                b = h * jblocks + j
                cut = slice(b * LANES, (b + 1) * LANES)
                turned.append(turn((vals[0, 0, here, cut], vals[1, 0, here, cut]), h))
            split(odd, turned, j, here, below)

    load_tab.wait()

    def give(k, d):
        to = lax.rem(win + d, nwin)
        return pltpu.make_async_remote_copy(
            src_ref=part.at[k, to], dst_ref=come.at[d - 1, k], send_sem=s3.at[k, d - 1],
            recv_sem=r3.at[k, d - 1], device_id=(chan, to), device_id_type=MESH)

    def lags(k, folded):
        r = lax.dot_general(tab[k], folded, (((1,), (1,)), ((), ())),
                            preferred_element_type=jnp.float32)
        low = r[:steps, rows:] + r[steps:, :rows] + r[steps:, rows:]
        part[k] = (r[:steps, :rows] + low).reshape(nwin, mine_steps, rows)
        for d in range(1, nwin):
            give(k, d).start()

    groups_each = rows // PACK // FOLD

    @pl.loop(0, FOLD)
    def _(m):
        lags(2 * m, even[m])
        for i in range(groups_each):
            fold_odd(m * groups_each + i)

    @pl.loop(0, FOLD)
    def _(m):
        lags(2 * m + 1, odd[m])

    for d in range(1, NEAR):
        scatter(d).wait_send()
        gather(d).wait_send()
    for d in range(1, nfar):
        across(d).wait_send()

    for k in range(CLASSES):
        value = part[k, win]
        for d in range(1, nwin):
            give(k, d).wait_recv()
            value = value + come[d - 1, k]
        acc[pl.ds(k, mine_steps, stride=CLASSES), :] = value

    for t in range(L // nwin // LANES):
        cut = slice(t * LANES, (t + 1) * LANES)
        out_ref[:, cut] = acc[cut, :].T

    @pl.loop(0, CLASSES)
    def _(k):
        for d in range(1, nwin):
            give(k, d).wait_send()


def body(spectra, exponents, source_channels):
    nch, nwin = lax.axis_size("chan"), lax.axis_size("win")
    _, segs, rows, nbin = spectra.shape
    per = 2 * segs * nbin // LANES // NEAR
    steps = L // CLASSES
    width = nbin // FOLD
    tables = jnp.asarray(lag_tables(nbin, 1.0 / math.sqrt(4.0 * nbin * segs * nwin)))
    f32, bf16, dma = jnp.float32, jnp.bfloat16, pltpu.SemaphoreType.DMA
    call = pl.pallas_call(
        functools.partial(kernel, nch, nwin),
        out_shape=jax.ShapeDtypeStruct((rows, L // nwin), f32),
        in_specs=[
            pl.BlockSpec(memory_space=pltpu.SMEM),
            pl.BlockSpec(memory_space=pl.ANY),
            pl.BlockSpec(memory_space=pl.ANY),
            pl.BlockSpec(memory_space=pl.ANY),
        ],
        out_specs=pl.BlockSpec(memory_space=pltpu.VMEM),
        scratch_shapes=[
            pltpu.VMEM(spectra.shape, bf16),
            pltpu.VMEM((CLASSES, 2 * steps, 2 * width), bf16),
            pltpu.VMEM(spectra.shape, f32),
            pltpu.VMEM((segs, nbin // LANES, rows), jnp.int32),
            pltpu.VMEM((rows, LANES), f32),
            pltpu.VMEM((NEAR, per, LANES), f32),
            pltpu.VMEM((NEAR, per, LANES), f32),
            pltpu.VMEM((per, LANES), f32),
            pltpu.VMEM((nch // NEAR, per, LANES), f32),
            pltpu.VMEM((per, LANES), f32),
            pltpu.VMEM((NEAR, per, LANES), f32),
            pltpu.VMEM((FOLD, 2 * rows, 2 * width), bf16),
            pltpu.VMEM((FOLD, 2 * rows, 2 * width), bf16),
            pltpu.VMEM((CLASSES, nwin, steps // nwin, rows), f32),
            pltpu.VMEM((nwin - 1, CLASSES, steps // nwin, rows), f32),
            pltpu.VMEM((L // nwin, rows), f32),
            dma, dma, dma,
            dma((NEAR,)), dma((NEAR,)), dma((nch // NEAR,)), dma((nch // NEAR,)), dma((NEAR,)), dma((NEAR,)),
            dma((CLASSES, nwin - 1)), dma((CLASSES, nwin - 1)),
        ],
        compiler_params=pltpu.CompilerParams(
            collective_id=0, has_side_effects=True, vmem_limit_bytes=60 * 2**20),
    )
    out = [call(source_channels[s : s + 1], jnp.swapaxes(exponents, 1, 2), spectra, tables)
           for s in range(source_channels.shape[0])]
    return jnp.stack(out)


def solution(mesh):
    return jax.shard_map(
        body,
        mesh=mesh,
        in_specs=(P(None, "win", "chan", None), P("win", "chan", None), P()),
        out_specs=P(None, "chan", "win"),
        check_vma=False,
    )
```

time: 38.7 us -> 36.3 us (0.938)
  local copies, waits for them, and re-layouts: 3.84 us -> 1.89 us
  Pallas kernels: 33.9 us -> 33.5 us
    unnamed x4 -> x1, local copies, waits for them, and re-layouts: 3.84 us -> 1.89 us
    pallas_call x1, Pallas kernels: 33.9 us -> 33.5 us  [body(): call(source_channels[s:s + 1], jnp.swapaxes(exponents, 1, 2), spectra, ta...]
where the time goes in v1:
time: 36.3 us; the launch traced here: 36.1 us
  Pallas kernels  33.5 us (92%)
  local copies, waits for them, and re-layouts  1.89 us (5%)
  between operations  0.66 us (2%)
    pallas_call x1, Pallas kernels, body(): call(source_channels[s:s + 1], jnp.swapaxes(exponents, 1, 2), spectra, ta...  33.5 us
    unnamed x1, local copies, waits for them, and re-layouts  1.89 us

profile of v1, /device:TPU:0, one launch (start us, length us, event | category | flops | bytes accessed | tf_op | source)
XLA Modules:
  0.0 36.1 jit_solution(14715662287043621501)
XLA Ops:
  0.7 33.5 %shard_map.46 = f32[128,1024]{1,0:T(8,128)} custom-call(s32[1]{0:T(128)S(6)} %copy.6.src_ref, s32[2,32,128]{2,1,0:T(8,128)} %bitcast.3, bf16[2,2,128,4096]{3,2,1,0:T(8,128)(2,1)} %spec_hbm.1, bf16[16,256,1024]{2,1,0:T(8,128)(2,1)} %constant.2.clone.tab_hbm), custom_call_target="tpu_custom_call" | custom-call | tf_op jit(solution)/shard_map/pallas_call | solution.py:317
  34.2 1.9 %copy.7 = f32[1,128,1024]{2,1,0:T(8,128)} copy(f32[1,128,1024]{2,1,0:T(8,128)} %bitcast.2) | data formatting | bytes 1048576

commit v2 on v1

--- a/solution.py
+++ b/solution.py
@@ -78,8 +78,11 @@
 
     load_exp = pltpu.make_async_copy(exp_hbm, raw, exp_sem)
     load_exp.start()
-    load = pltpu.make_async_copy(spec_hbm, spec, spec_sem)
-    load.start()
+    loads = [
+        [pltpu.make_async_copy(spec_hbm.at[plane, g], spec.at[plane, g], spec_sem.at[plane, g])
+         for g in range(segs)] for plane in range(2)]
+    for load in loads[0] + loads[1]:
+        load.start()
     load_tab = pltpu.make_async_copy(tab_hbm, tab, tab_sem)
 
     near, far = lax.rem(chan, NEAR), lax.div(chan, NEAR)
@@ -107,18 +110,29 @@
     flat = jnp.exp2(raw[...].astype(jnp.float32)).reshape(segs * blocks, rows)
     square = jnp.concatenate([flat, jnp.ones((LANES - segs * blocks, rows), jnp.float32)], axis=0)
     scales[...] = square.T
-    load.wait()
-    load_tab.start()
     local = src_ref[0] - chan * rows
     line = lax.broadcasted_iota(jnp.int32, (rows, LANES), 0)
     hits = (line == local).astype(jnp.float32)
     groups = rows // PACK
     marks = [hits[i * PACK : (i + 1) * PACK].astype(jnp.bfloat16) for i in range(groups)]
+    def scatter(d):
+        to = beside(d)
+        return pltpu.make_async_remote_copy(
+            src_ref=pick.at[to], dst_ref=got.at[d], send_sem=s1.at[d], recv_sem=r1.at[d],
+            device_id=(far * NEAR + to, win), device_id_type=MESH)
+
+    def send(piece):
+        @pl.when(near != piece)
+        def _():
+            scatter(lax.rem(piece - near + NEAR, NEAR)).start()
+
     scale = jnp.sum(scales[...] * hits, axis=0, keepdims=True)
-    for g in range(segs):
-        for b in range(blocks):
-            wide = jnp.broadcast_to(scale[:, g * blocks + b : g * blocks + b + 1], (1, LANES))
-            for plane in range(2):
+    sent = 0
+    for plane in range(2):
+        for g in range(segs):
+            loads[plane][g].wait()
+            for b in range(blocks):
+                wide = jnp.broadcast_to(scale[:, g * blocks + b : g * blocks + b + 1], (1, LANES))
                 x = None
                 for i in range(groups):
                     y = spec[plane, g, i * PACK : (i + 1) * PACK, b * LANES : (b + 1) * LANES] * marks[i]
@@ -126,14 +140,13 @@
                 row = (plane * segs + g) * blocks + b
                 one = jnp.sum(x.astype(jnp.float32), axis=0, keepdims=True)
                 pick[row // per, row % per : row % per + 1, :] = one * wide
-
-    pl.semaphore_wait(barrier, NEAR + nfar + nwin - 3)
-
-    def scatter(d):
-        to = beside(d)
-        return pltpu.make_async_remote_copy(
-            src_ref=pick.at[to], dst_ref=got.at[d], send_sem=s1.at[d], recv_sem=r1.at[d],
-            device_id=(far * NEAR + to, win), device_id_type=MESH)
+            if plane == 0 and g == 0:
+                pl.semaphore_wait(barrier, NEAR + nfar + nwin - 3)
+            done = ((plane * segs + g) + 1) * blocks // per
+            for piece in range(sent, done):
+                send(piece)
+            sent = done
+    load_tab.start()
 
     def across(d):
         return pltpu.make_async_remote_copy(
@@ -145,8 +158,6 @@
             src_ref=total, dst_ref=slab.at[near], send_sem=s4.at[d], recv_sem=r4.at[d],
             device_id=(far * NEAR + beside(d), win), device_id_type=MESH)
 
-    for d in range(1, NEAR):
-        scatter(d).start()
     added = pick[near]
     for d in range(1, NEAR):
         scatter(d).wait_recv()
@@ -307,7 +318,7 @@
             pltpu.VMEM((CLASSES, nwin, steps // nwin, rows), f32),
             pltpu.VMEM((nwin - 1, CLASSES, steps // nwin, rows), f32),
             pltpu.VMEM((L // nwin, rows), f32),
-            dma, dma, dma,
+            dma((2, segs)), dma, dma,
             dma((NEAR,)), dma((NEAR,)), dma((nch // NEAR,)), dma((nch // NEAR,)), dma((NEAR,)), dma((NEAR,)),
             dma((CLASSES, nwin - 1)), dma((CLASSES, nwin - 1)),
         ],

time: 36.3 us -> 35.6 us (0.981)
  Pallas kernels: 33.5 us -> 32.9 us
    pallas_call x1, Pallas kernels: 33.5 us -> 32.9 us  [body(): call(source_channels[s:s + 1], jnp.swapaxes(exponents, 1, 2), spectra, ta...]
where the time goes in v2:
time: 35.6 us; the launch traced here: 35.4 us
  Pallas kernels  32.9 us (92%)
  local copies, waits for them, and re-layouts  1.89 us (5%)
  between operations  0.66 us (2%)
    pallas_call x1, Pallas kernels, body(): call(source_channels[s:s + 1], jnp.swapaxes(exponents, 1, 2), spectra, ta...  32.9 us
    unnamed x1, local copies, waits for them, and re-layouts  1.89 us

profile of v2, /device:TPU:0, one launch (start us, length us, event | category | flops | bytes accessed | tf_op | source)
XLA Modules:
  0.0 35.4 jit_solution(13430991471560594250)
XLA Ops:
  0.7 32.9 %shard_map.46 = f32[128,1024]{1,0:T(8,128)} custom-call(s32[1]{0:T(128)S(6)} %copy.6.src_ref, s32[2,32,128]{2,1,0:T(8,128)} %bitcast.3, bf16[2,2,128,4096]{3,2,1,0:T(8,128)(2,1)} %spec_hbm.1, bf16[16,256,1024]{2,1,0:T(8,128)(2,1)} %constant.2.clone.tab_hbm), custom_call_target="tpu_custom_call" | custom-call | tf_op jit(solution)/shard_map/pallas_call | solution.py:328
  33.5 1.9 %copy.7 = f32[1,128,1024]{2,1,0:T(8,128)} copy(f32[1,128,1024]{2,1,0:T(8,128)} %bitcast.2) | data formatting | bytes 1048576

commit v3 on v2

--- a/solution.py
+++ b/solution.py
@@ -65,7 +65,7 @@
 
 def kernel(nch, nwin, src_ref, exp_hbm, spec_hbm, tab_hbm, out_ref,
            spec, tab, vals, raw, scales, pick, got, mine, got2, total, slab, even, odd,
-           part, come, acc,
+           part, come,
            spec_sem, tab_sem, exp_sem, s1, r1, s2, r2, s4, r4, s3, r3):
     chan, win = lax.axis_index("chan"), lax.axis_index("win")
     segs, rows, nbin = spec.shape[1], spec.shape[2], spec.shape[3]
@@ -271,11 +271,7 @@
         for d in range(1, nwin):
             give(k, d).wait_recv()
             value = value + come[d - 1, k]
-        acc[pl.ds(k, mine_steps, stride=CLASSES), :] = value
-
-    for t in range(L // nwin // LANES):
-        cut = slice(t * LANES, (t + 1) * LANES)
-        out_ref[:, cut] = acc[cut, :].T
+        out_ref[pl.ds(k, mine_steps, stride=CLASSES), :] = value
 
     @pl.loop(0, CLASSES)
     def _(k):
@@ -293,7 +289,7 @@
     f32, bf16, dma = jnp.float32, jnp.bfloat16, pltpu.SemaphoreType.DMA
     call = pl.pallas_call(
         functools.partial(kernel, nch, nwin),
-        out_shape=jax.ShapeDtypeStruct((rows, L // nwin), f32),
+        out_shape=jax.ShapeDtypeStruct((L // nwin, rows), f32),
         in_specs=[
             pl.BlockSpec(memory_space=pltpu.SMEM),
             pl.BlockSpec(memory_space=pl.ANY),
@@ -317,7 +313,6 @@
             pltpu.VMEM((FOLD, 2 * rows, 2 * width), bf16),
             pltpu.VMEM((CLASSES, nwin, steps // nwin, rows), f32),
             pltpu.VMEM((nwin - 1, CLASSES, steps // nwin, rows), f32),
-            pltpu.VMEM((L // nwin, rows), f32),
             dma((2, segs)), dma, dma,
             dma((NEAR,)), dma((NEAR,)), dma((nch // NEAR,)), dma((nch // NEAR,)), dma((NEAR,)), dma((NEAR,)),
             dma((CLASSES, nwin - 1)), dma((CLASSES, nwin - 1)),
@@ -327,7 +322,7 @@
     )
     out = [call(source_channels[s : s + 1], jnp.swapaxes(exponents, 1, 2), spectra, tables)
            for s in range(source_channels.shape[0])]
-    return jnp.stack(out)
+    return jnp.stack([lagged.T for lagged in out])
 
 
 def solution(mesh):

time: 35.6 us -> 35.5 us (level)
    another operation x0 -> x1, local copies, waits for them, and re-layouts: none -> 2.04 us  [body(): return jnp.stack([lagged.T for lagged in out])]
    unnamed x1 -> x0, local copies, waits for them, and re-layouts: 1.89 us -> none
where the time goes in v3:
time: 35.5 us; the launch traced here: 35.4 us
  Pallas kernels  32.7 us (92%)
  local copies, waits for them, and re-layouts  2.04 us (6%)
  between operations  0.66 us (2%)
    pallas_call x1, Pallas kernels, body(): call(source_channels[s:s + 1], jnp.swapaxes(exponents, 1, 2), spectra, ta...  32.7 us
    another operation x1, local copies, waits for them, and re-layouts, body(): return jnp.stack([lagged.T for lagged in out])  2.04 us

profile of v3, /device:TPU:0, one launch (start us, length us, event | category | flops | bytes accessed | tf_op | source)
XLA Modules:
  0.0 35.4 jit_solution(3814958252034346164)
XLA Ops:
  0.7 32.7 %shard_map.46 = f32[1024,128]{1,0:T(8,128)} custom-call(s32[1]{0:T(128)S(6)} %copy.6.src_ref, s32[2,32,128]{2,1,0:T(8,128)} %bitcast.5, bf16[2,2,128,4096]{3,2,1,0:T(8,128)(2,1)} %spec_hbm.1, bf16[16,256,1024]{2,1,0:T(8,128)(2,1)} %constant.2.clone.tab_hbm), custom_call_target="tpu_custom_call" | custom-call | tf_op jit(solution)/shard_map/pallas_call | solution.py:323
  33.3 2.0 %copy.5 = f32[1,128,1024]{2,1,0:T(8,128)} copy(f32[1,128,1024]{1,2,0:T(8,128)} %bitcast.4) | data formatting | bytes 1048576 | tf_op jit(solution)/shard_map/stack | solution.py:325
